TPU v7x, 128 devices: a whole 4x4x4 slice. The times are simulated.
128 devices in a mesh: tile: 16 (over z_lo, y, core), lev: 8 (over x, z_hi).
Axes of the slice: x: 4, y: 4, z: 4 (z_hi: 2, z_lo: 2; z = z_hi * 2 + z_lo), core: 2. Of those that a mesh axis runs over, the one named last changes fastest.
Arguments:
- adjoint_state: float32 [4, 88, 1024, 256], P(None, 'lev', 'tile'), may hold values from -6 to 6
- lower_coef: float32 [88, 1024, 256], P('lev', 'tile'), may hold values from 0.1 to 10
- upper_coef: float32 [88, 1024, 256], P('lev', 'tile'), may hold values from 0.1 to 10
- stencil_coef: float32 [4, 1024, 256], P(None, 'tile'), may hold values from 0.02 to 0.24
- land_mask: int32 [1024, 256], P('tile'), may hold values 0 or 1
Outputs:
- adjoint_input: float32 [4, 88, 1024, 256], P(None, 'lev', 'tile')
All inputs are finite; a program needn't handle non-finite values. No bound on the sum of `land_mask` on one device may be relied on, other than what follows from the above.
Results may differ from a plain program's by a relative error of at most 0.00002.
Values sent between devices are 32-bit elements; how exact they have to be, the bound alone decides.
A program may use at most 256 MiB of HBM per device.

v0:
```python
import functools

import jax
import jax.numpy as jnp
from jax import lax
from jax.experimental import pallas as pl
from jax.experimental.pallas import tpu as pltpu
from jax.sharding import PartitionSpec as P

MESH = pl.DeviceIdType.MESH
N = 8
FIELDS = 4
LEVELS = 11
ROWS, COLS = 64, 256
LANES = 128
PAD = 8
HEIGHT = ROWS + 2 * PAD
STACK = FIELDS * LEVELS
QUARTER = 16
PLANES = 4 + 2 * FIELDS
BACK = 2 * FIELDS
FORWARD = (slice(0, 1 + FIELDS), slice(0, PLANES), slice(PLANES - 1 - FIELDS, PLANES))
BACKWARD = (slice(FIELDS, BACK), slice(0, BACK), slice(0, FIELDS))


def quarter_row(i):
    return pl.multiple_of(QUARTER * lax.rem(3 * i, 4), QUARTER)


def solver(group, j):
    return 2 * j + lax.rem(group + j, 2)


def spot(fk, c, r):
    return (fk * 2 + c) * HEIGHT + PAD + r


def transport(x_v, co_v, out, start, to):
    start, to = pl.multiple_of(start, QUARTER), pl.multiple_of(to, QUARTER)
    lane = lax.broadcasted_iota(jnp.int32, (QUARTER, LANES), 1)
    co = [[co_v[n, c, pl.ds(start, QUARTER), :] for c in range(2)] for n in range(5)]

    def one(fk, carry):
        f, k = lax.div(fk, LEVELS), lax.rem(fk, LEVELS)
        at = [pl.multiple_of(spot(fk, c, start), 8) for c in range(2)]
        x = [x_v[pl.ds(at[c], QUARTER), :] for c in range(2)]
        up = [x_v[pl.ds(at[c] - 1, QUARTER), :] for c in range(2)]
        down = [x_v[pl.ds(at[c] + 1, QUARTER), :] for c in range(2)]
        fwd = [pltpu.roll(x[c], 1, 1) for c in range(2)]
        bwd = [pltpu.roll(x[c], LANES - 1, 1) for c in range(2)]
        fwd[1] = jnp.where(lane == 0, fwd[0], fwd[1])
        bwd[0] = jnp.where(lane == LANES - 1, bwd[1], bwd[0])
        for c in range(2):
            total = x[c] * co[0][c] + up[c] * co[1][c] + down[c] * co[2][c]
            total = total + fwd[c] * co[3][c] + bwd[c] * co[4][c]
            out[f, k, pl.ds(to, QUARTER), pl.ds(c * LANES, LANES)] = total
        return carry

    return lax.fori_loop(0, STACK, one, 0, unroll=STACK)


def finish(x_v, co_v, hr, part, out, o_v, sem):
    def store(ref, start, to, n):
        return pltpu.make_async_copy(
            ref.at[:, :, pl.ds(start, QUARTER), :], out.at[:, :, pl.ds(to, QUARTER), :], sem.at[n])

    last = ROWS - QUARTER
    copies = [store(part, 2 * QUARTER, QUARTER, 0), store(o_v, 0, 0, 1), store(o_v, last, last, 2),
              store(o_v, 2 * QUARTER, 2 * QUARTER, 3)]
    copies[0].start()
    row = lax.broadcasted_iota(jnp.int32, (8, LANES), 0)
    for n, (start, to, rows) in enumerate(((0, 0, (None, QUARTER)), (QUARTER, last, (last - 1, None)))):
        weight = [[jnp.where(row == r, co_v[1 + i, c, pl.ds(to + 8 * i, 8), :], 0.0) for c in range(2)]
                  for i, r in ((0, 0), (1, 7))]

        def patch(fk, carry):
            f, k = lax.div(fk, LEVELS), lax.rem(fk, LEVELS)
            for c in range(2):
                cols = pl.ds(c * LANES, LANES)
                for i in range(2):
                    if rows[i] is None:
                        term = hr[i, c, pl.ds(fk, 1), :]
                    else:
                        term = x_v[pl.ds(spot(fk, c, rows[i]), 1), :]
                    o_v[f, k, pl.ds(to + 8 * i, 8), cols] = part[f, k, pl.ds(start + 8 * i, 8), cols] + weight[i][c] * term
            return carry

        lax.fori_loop(0, STACK, patch, 0, unroll=STACK)
        copies[1 + n].start()
    transport(x_v, co_v, o_v, 2 * QUARTER, 2 * QUARTER)
    copies[3].start()
    for copy in copies:
        copy.wait()


def kernel(
    adj, low, upp, sten, mask, x_v, co_v, hr, part,
    m_v, a_v, b_v, s_v, k_v, snd, rcv, rts, rtr, hs,
    load_sem, small_sem, fs, fr, fl, bs, br, bl, hss, hrs,
):
    tile = lax.axis_index("tile")
    lev = lax.axis_index("lev")
    tiles = lax.axis_size("tile")

    barrier = pltpu.get_barrier_semaphore()
    for off in range(1, N):
        pl.semaphore_signal(barrier, inc=1, device_id=(tile, lax.rem(lev + off, N)), device_id_type=MESH)
    right, left = lax.rem(tile + 1, tiles), lax.rem(tile + tiles - 1, tiles)
    for t in (right, left):
        pl.semaphore_signal(barrier, inc=1, device_id=(t, lev), device_id_type=MESH)

    def loads(i):
        rows = pl.ds(quarter_row(i), QUARTER)
        return (
            pltpu.make_async_copy(adj.at[:, :, rows, :], m_v.at[:, :, rows, :], load_sem.at[i, 0]),
            pltpu.make_async_copy(low.at[:, rows, :], a_v.at[:, rows, :], load_sem.at[i, 1]),
            pltpu.make_async_copy(upp.at[:, rows, :], b_v.at[:, rows, :], load_sem.at[i, 2]),
        )

    load_mask = pltpu.make_async_copy(mask, k_v, small_sem.at[0])
    load_sten = pltpu.make_async_copy(sten, s_v, small_sem.at[1])
    load_mask.start()
    for i in range(4):
        for c in loads(i):
            c.start()
    load_sten.start()

    @pl.when(lev == 0)
    def _():
        rtr[:, :, :FIELDS] = jnp.zeros((2, N, FIELDS, 8, LANES), jnp.float32)

    @pl.when(lev == N - 1)
    def _():
        rtr[:, :, FIELDS:] = jnp.zeros((2, N, FIELDS, 8, LANES), jnp.float32)

    first = jnp.where(lev == 0, 0.0, 1.0)
    last = jnp.where(lev == N - 1, 0.0, 1.0)

    def eliminate(i):
        for c in loads(i):
            c.wait()
        start = quarter_row(i)
        rows = pl.ds(start, QUARTER)
        half, group = lax.div(i, 2), lax.rem(i, 2)
        keep = k_v[rows, :].astype(jnp.float32)
        r = [None] * FIELDS
        p = [None] * FIELDS
        a = a_v[0, rows, :] * first
        chain = a
        inv = g = q = b = None
        for k in range(LEVELS):
            b_next = b_v[k, rows, :]
            if k == LEVELS - 1:
                b_next = b_next * last
            d = 1.0 + a + b_next
            if k:
                d = d - b * a * inv
            inv = pltpu.reciprocal(d, approx=True)
            if k:
                h = b * inv
                g = h * g
                q = q + chain * g
            else:
                g = inv
                q = chain * g
            for f in range(FIELDS):
                m = m_v[f, k, rows, :] * keep
                if k:
                    r[f] = m * inv + h * r[f]
                    p[f] = p[f] + chain * r[f]
                else:
                    r[f] = m * inv
                    p[f] = chain * r[f]
                m_v[f, k, rows, :] = r[f]
            if k < LEVELS - 1:
                a = a_v[k + 1, rows, :]
                e = a * inv
            else:
                e = inv
            chain = chain * e
            a_v[k, rows, :] = e
            b_v[k, rows, :] = g
            b = b_next
        planes = [b * inv] + [b * r[f] for f in range(FIELDS)] + [chain, b * g, q] + p
        for j in range(4):
            row, col = (j // 2) * 8, (j % 2) * LANES
            for n, plane in enumerate(planes):
                snd[half, solver(group, j), n] = plane[row:row + 8, col:col + LANES]

    def forward(half, to, part):
        return pltpu.make_async_remote_copy(
            src_ref=snd.at[half, to, part], dst_ref=rcv.at[half, lev, part], send_sem=fs.at[half, to],
            recv_sem=fr.at[half, lev], device_id=(tile, to), device_id_type=MESH)

    def forward_from(half, source, part):
        return pltpu.make_async_remote_copy(
            src_ref=snd.at[half, source, part], dst_ref=rcv.at[half, source, part], send_sem=fs.at[half, source],
            recv_sem=fr.at[half, source], device_id=(tile, source), device_id_type=MESH)

    def backward(half, to, part):
        return pltpu.make_async_remote_copy(
            src_ref=rts.at[half, to, part], dst_ref=rtr.at[half, lev, part], send_sem=bs.at[half, to],
            recv_sem=br.at[half, lev], device_id=(tile, to), device_id_type=MESH)

    def backward_from(half, source, part):
        return pltpu.make_async_remote_copy(
            src_ref=rts.at[half, source, part], dst_ref=rtr.at[half, source, part], send_sem=bs.at[half, source],
            recv_sem=br.at[half, source], device_id=(tile, source), device_id_type=MESH)

    def own_forward(half):
        return pltpu.make_async_copy(snd.at[half, lev], rcv.at[half, lev], fl.at[half])

    def own_backward(half):
        return pltpu.make_async_copy(rts.at[half, lev], rtr.at[half, lev], bl.at[half])

    def by_slab(s, parts, run):
        pl.when(s == 0)(lambda: run(parts[0]))
        pl.when(s == N - 1)(lambda: run(parts[2]))
        pl.when((s != 0) & (s != N - 1))(lambda: run(parts[1]))

    def send_forward(i):
        half, group = lax.div(i, 2), lax.rem(i, 2)

        def run(part):
            for j in range(4):
                to = solver(group, j)
                pl.when(to != lev)(lambda: forward(half, to, part).start())

        by_slab(lev, FORWARD, run)
        for j in range(4):
            pl.when(solver(group, j) == lev)(lambda: own_forward(half).start())

    def quarter(i, carry):
        eliminate(i)
        pl.when(i == 0)(lambda: pl.semaphore_wait(barrier, N + 1))
        send_forward(i)
        return carry

    load_mask.wait()
    lax.fori_loop(0, 4, quarter, 0)
    load_sten.wait()

    row = lax.broadcasted_iota(jnp.int32, (ROWS, LANES), 0)
    lane = lax.broadcasted_iota(jnp.int32, (ROWS, LANES), 1)
    has_left = jnp.where(tile == 0, 0.0, 1.0)
    has_right = jnp.where(tile == tiles - 1, 0.0, 1.0)
    for c in range(2):
        cols = pl.ds(c * LANES, LANES)
        east, west, north, south = s_v[0, :, cols], s_v[1, :, cols], s_v[2, :, cols], s_v[3, :, cols]
        co_v[0, c] = 1.0 - (east + west + north + south)
        co_v[1, c] = jnp.where(row == 0, has_left, pltpu.roll(east, 1, 0))
        co_v[2, c] = jnp.where(row == ROWS - 1, has_right, pltpu.roll(west, ROWS - 1, 0))
        before = 0.0 if c == 0 else pltpu.roll(s_v[2, :, :LANES], 1, 1)
        after = pltpu.roll(s_v[3, :, LANES:], LANES - 1, 1) if c == 0 else 0.0
        co_v[3, c] = jnp.where(lane == 0, before, pltpu.roll(north, 1, 1))
        co_v[4, c] = jnp.where(lane == LANES - 1, after, pltpu.roll(south, LANES - 1, 1))

    def clear(n, carry):
        for r in (-PAD, QUARTER, ROWS - QUARTER - 8, ROWS):
            x_v[pl.ds(pl.multiple_of(n * HEIGHT + PAD + r, 8), 8), :] = jnp.zeros((8, LANES), jnp.float32)
        return carry

    lax.fori_loop(0, 2 * STACK, clear, 0, unroll=8)

    def solve(half, carry):
        own_forward(half).wait()
        for s in range(N):
            part = FORWARD[0 if s == 0 else 2 if s == N - 1 else 1]
            pl.when(lev != s)(lambda: forward_from(half, s, part).wait_recv())
        fields = range(FIELDS)
        flux = [rcv[half, 0, 1 + f] for f in fields]
        slope = rcv[half, 0, 0]
        into, gain = [None] * N, [None] * N
        for s in range(1, N):
            aa = rcv[half, s, 7]
            inv = pltpu.reciprocal(1.0 - slope * aa, approx=True)
            into[s] = [(flux[f] + slope * rcv[half, s, 8 + f]) * inv for f in fields]
            if s < N - 1:
                dd, bb, cc = rcv[half, s, 0], rcv[half, s, 5], rcv[half, s, 6]
                gain[s] = slope * bb * inv
                flux = [rcv[half, s, 1 + f] + cc * into[s][f] for f in fields]
                slope = dd + cc * gain[s]
        zero = jnp.zeros((8, LANES), jnp.float32)
        v = [zero] * FIELDS
        for s in range(N - 1, -1, -1):
            if s == 0:
                u = [zero] * FIELDS
            elif s == N - 1:
                u = into[s]
            else:
                u = [into[s][f] + gain[s] * v[f] for f in fields]
            for f in fields:
                rts[half, s, f] = u[f]
                rts[half, s, FIELDS + f] = v[f]
            if s:
                w = [rcv[half, s, 8 + f] + rcv[half, s, 7] * u[f] for f in fields]
                v = w if s == N - 1 else [w[f] + rcv[half, s, 5] * v[f] for f in fields]
        own_backward(half).start()
        for off in range(1, N):
            to = lax.rem(lev + off, N)
            by_slab(to, BACKWARD, lambda part: backward(half, to, part).start())
        return carry

    lax.fori_loop(0, 2, solve, 0)

    def returned(half):
        own_backward(half).wait()

        def run(part):
            for off in range(1, N):
                backward_from(half, lax.rem(lev + off, N), part).wait_recv()

        by_slab(lev, BACKWARD, run)

    def substitute(half, j):
        start = pl.multiple_of(quarter_row(half * 2 + lax.div(j, 2)) + 8 * lax.rem(j, 2), 8)
        rows = pl.ds(start, 8)
        for c in range(2):
            cols = pl.ds(c * LANES, LANES)
            source = solver(lax.div(j, 2), 2 * lax.rem(j, 2) + c)
            x = [None] * FIELDS
            for k in range(LEVELS - 1, -1, -1):
                e, g = a_v[k, rows, cols], b_v[k, rows, cols]
                for f in range(FIELDS):
                    u = rtr[half, source, f]
                    beyond = rtr[half, source, FIELDS + f] if k == LEVELS - 1 else x[f]
                    x[f] = m_v[f, k, rows, cols] + g * u + e * beyond
                    x_v[pl.ds(pl.multiple_of(spot(f * LEVELS + k, c, start), 8), 8), :] = x[f]

    def halo(way):
        to = right if way == 0 else left
        return pltpu.make_async_remote_copy(
            src_ref=hs.at[way], dst_ref=hr.at[way], send_sem=hss.at[way], recv_sem=hrs.at[way],
            device_id=(to, lev), device_id_type=MESH)

    def every(c, r):
        return pl.ds(spot(0, c, r), STACK, stride=2 * HEIGHT)

    def blocks(half, first, count, step):
        def body(n, carry):
            substitute(half, first + n * step)
            return carry

        lax.fori_loop(0, count, body, 0, unroll=2)

    returned(0)
    blocks(0, 0, 2, 3)
    for way, r in ((0, ROWS - 1), (1, 0)):
        for c in range(2):
            weight = s_v[way, r:r + 1, c * LANES:(c + 1) * LANES]
            hs[way, c] = x_v[every(c, r), :] * weight
        halo(way).start()
    blocks(0, 1, 2, 1)
    lax.fori_loop(0, 2, lambda j, carry: transport(x_v, co_v, part, j * (ROWS - QUARTER), j * QUARTER), 0)
    returned(1)
    blocks(1, 0, 4, 1)
    transport(x_v, co_v, part, QUARTER, 2 * QUARTER)
    for way in range(2):
        halo(way).wait()

    def drain(part):
        for half in range(2):
            for off in range(1, N):
                forward(half, lax.rem(lev + off, N), part).wait_send()

    by_slab(lev, FORWARD, drain)
    for half in range(2):
        for off in range(1, N):
            to = lax.rem(lev + off, N)
            by_slab(to, BACKWARD, lambda part: backward(half, to, part).wait_send())


def per_device(adjoint_state, lower_coef, upper_coef, stencil_coef, land_mask):
    f32 = jnp.float32
    dma = pltpu.SemaphoreType.DMA
    space = pltpu.VMEM
    fields, slab, rows, cols = adjoint_state.shape
    parts = pl.pallas_call(
        kernel,
        out_shape=[
            space((STACK * 2 * HEIGHT, LANES), f32),
            space((5, 2, ROWS, LANES), f32),
            space((2, 2, STACK, LANES), f32),
            space((fields, slab, 3 * QUARTER, cols), f32),
        ],
        in_specs=[pl.BlockSpec(memory_space=pltpu.HBM)] * 5,
        out_specs=[pl.BlockSpec(memory_space=space)] * 4,
        scratch_shapes=[
            space((FIELDS, LEVELS, ROWS, COLS), f32),
            space((LEVELS, ROWS, COLS), f32),
            space((LEVELS, ROWS, COLS), f32),
            space((4, ROWS, COLS), f32),
            space((ROWS, COLS), jnp.int32),
            space((2, N, PLANES, 8, LANES), f32),
            space((2, N, PLANES, 8, LANES), f32),
            space((2, N, BACK, 8, LANES), f32),
            space((2, N, BACK, 8, LANES), f32),
            space((2, 2, STACK, LANES), f32),
            dma((4, 3)),
            dma((2,)),
            dma((2, N)),
            dma((2, N)),
            dma((2,)),
            dma((2, N)),
            dma((2, N)),
            dma((2,)),
            dma((2,)),
            dma((2,)),
        ],
        compiler_params=pltpu.CompilerParams(
            collective_id=0, has_side_effects=True, vmem_limit_bytes=32 * 2**20),
    )(*(pltpu.with_memory_space_constraint(x, pltpu.HBM) for x in (
        adjoint_state, lower_coef, upper_coef, stencil_coef, land_mask)))
    return pl.pallas_call(
        finish,
        out_shape=jax.ShapeDtypeStruct(adjoint_state.shape, f32),
        in_specs=[pl.BlockSpec(memory_space=space)] * 4,
        out_specs=pl.BlockSpec(memory_space=pltpu.HBM),
        scratch_shapes=[space(adjoint_state.shape, f32), dma((4,))],
        compiler_params=pltpu.CompilerParams(vmem_limit_bytes=16 * 2**20),
    )(*(pltpu.with_memory_space_constraint(x, space) for x in parts))


def solution(mesh):
    return jax.shard_map(
        per_device,
        mesh=mesh,
        in_specs=(
            P(None, "lev", "tile", None),
            P("lev", "tile", None),
            P("lev", "tile", None),
            P(None, "tile", None),
            P("tile", None),
        ),
        out_specs=P(None, "lev", "tile", None),
        check_vma=False,
    )
```

profile of v0, /device:TPU:1, one launch (start us, length us, event | category | flops | bytes accessed | tf_op | source)
XLA Modules:
  0.0 27.0 jit_solution(13941488829906932068)
XLA Ops:
  0.0 25.4 %shard_map.55 = (f32[7040,128]{1,0:T(8,128)S(1)}, f32[5,2,64,128]{3,2,1,0:T(8,128)S(1)}, f32[2,2,44,128]{3,2,1,0:T(8,128)S(1)}, f32[4,11,48,256]{3,2,1,0:T(8,128)S(1)}) custom-call(f32[4,11,64,256]{3,2,1,0:T(8,128)} %adj.1, f32[11,64,256]{2,1,0:T(8,128)} %low.1, f32[11,64,256]{2,1,0:T(8,128)} %upp.1, f32[4,64,256]{2,1,0:T(8,128)} %sten.1, s32[64,256]{1,0:T(8,128)} %mask.1), custom_call_target="tpu_custom_call" | custom-call | tf_op jit(solution)/shard_map/pallas_call | solution.py:378
  25.4 1.6 %shard_map.56 = f32[4,11,64,256]{3,2,1,0:T(8,128)} custom-call(f32[7040,128]{1,0:T(8,128)S(1)} %get-tuple-element.9.x_v, f32[5,2,64,128]{3,2,1,0:T(8,128)S(1)} %get-tuple-element.10.co_v, f32[2,2,44,128]{3,2,1,0:T(8,128)S(1)} %get-tuple-element.11.hr, f32[4,11,48,256]{3,2,1,0:T(8,128)S(1)} %get-tuple-element.12.part), custom_call_target="tpu_custom_call" | custom-call | tf_op jit(solution)/shard_map/pallas_call | solution.py:414
where the time goes:
time: 27.5 us; the launch traced here: 27 us
  Pallas kernels  27 us (98%)
    pallas_call x1, Pallas kernels, per_device(): pl.pallas_call(kernel, out_shape=[space((STACK * 2 * HEIGHT, LANES), f32)...  25.4 us
    pallas_call x1, Pallas kernels, per_device(): pl.pallas_call(finish, out_shape=jax.ShapeDtypeStruct(adjoint_state.shape...  1.61 us

commit v1 on v0

--- a/solution.py
+++ b/solution.py
@@ -222,18 +222,17 @@
         half, group = lax.div(i, 2), lax.rem(i, 2)
 
         def run(part):
-            for j in range(4):
-                to = solver(group, j)
-                pl.when(to != lev)(lambda: forward(half, to, part).start())
+            for dx, dz in ((2, 1), (1, 1), (3, 1), (0, 1), (2, 0), (1, 0), (3, 0)):
+                to = 2 * lax.rem(lax.div(lev, 2) + dx, 4) + lax.rem(lev + dz, 2)
+                forward(half, to, part).start()
 
         by_slab(lev, FORWARD, run)
-        for j in range(4):
-            pl.when(solver(group, j) == lev)(lambda: own_forward(half).start())
+        own_forward(half).start()
 
     def quarter(i, carry):
         eliminate(i)
-        pl.when(i == 0)(lambda: pl.semaphore_wait(barrier, N + 1))
-        send_forward(i)
+        pl.when(i == 1)(lambda: pl.semaphore_wait(barrier, N + 1))
+        pl.when(lax.rem(i, 2) == 1)(lambda: send_forward(i))
         return carry
 
     load_mask.wait()
@@ -296,8 +295,8 @@
                 w = [rcv[half, s, 8 + f] + rcv[half, s, 7] * u[f] for f in fields]
                 v = w if s == N - 1 else [w[f] + rcv[half, s, 5] * v[f] for f in fields]
         own_backward(half).start()
-        for off in range(1, N):
-            to = lax.rem(lev + off, N)
+        for dx, dz in ((2, 1), (1, 1), (3, 1), (0, 1), (2, 0), (1, 0), (3, 0)):
+            to = 2 * lax.rem(lax.div(lev, 2) + dx, 4) + lax.rem(lev + dz, 2)
             by_slab(to, BACKWARD, lambda part: backward(half, to, part).start())
         return carry
 

time: 27.5 us -> 26.5 us (0.964); the launches traced: 27 us -> 26.4 us
  Pallas kernels: 27 us -> 26.3 us
    pallas_call x1, Pallas kernels: 25.4 us -> 24.7 us  [per_device(): pl.pallas_call(kernel, out_shape=[space((STACK * 2 * HEIGHT, LANES), f32)...]
where the time goes in v1:
time: 26.5 us; the launch traced here: 26.4 us
  Pallas kernels  26.3 us (99%)
    pallas_call x1, Pallas kernels, per_device(): pl.pallas_call(kernel, out_shape=[space((STACK * 2 * HEIGHT, LANES), f32)...  24.7 us
    pallas_call x1, Pallas kernels, per_device(): pl.pallas_call(finish, out_shape=jax.ShapeDtypeStruct(adjoint_state.shape...  1.61 us

profile of v1, /device:TPU:1, one launch (start us, length us, event | category | flops | bytes accessed | tf_op | source)
XLA Modules:
  0.0 26.4 jit_solution(5797986088050137248)
XLA Ops:
  0.0 24.7 %shard_map.55 = (f32[7040,128]{1,0:T(8,128)S(1)}, f32[5,2,64,128]{3,2,1,0:T(8,128)S(1)}, f32[2,2,44,128]{3,2,1,0:T(8,128)S(1)}, f32[4,11,48,256]{3,2,1,0:T(8,128)S(1)}) custom-call(f32[4,11,64,256]{3,2,1,0:T(8,128)} %adj.1, f32[11,64,256]{2,1,0:T(8,128)} %low.1, f32[11,64,256]{2,1,0:T(8,128)} %upp.1, f32[4,64,256]{2,1,0:T(8,128)} %sten.1, s32[64,256]{1,0:T(8,128)} %mask.1), custom_call_target="tpu_custom_call" | custom-call | tf_op jit(solution)/shard_map/pallas_call | solution.py:377
  24.7 1.6 %shard_map.56 = f32[4,11,64,256]{3,2,1,0:T(8,128)} custom-call(f32[7040,128]{1,0:T(8,128)S(1)} %get-tuple-element.9.x_v, f32[5,2,64,128]{3,2,1,0:T(8,128)S(1)} %get-tuple-element.10.co_v, f32[2,2,44,128]{3,2,1,0:T(8,128)S(1)} %get-tuple-element.11.hr, f32[4,11,48,256]{3,2,1,0:T(8,128)S(1)} %get-tuple-element.12.part), custom_call_target="tpu_custom_call" | custom-call | tf_op jit(solution)/shard_map/pallas_call | solution.py:413

commit v2 on v1

--- a/solution.py
+++ b/solution.py
@@ -29,6 +29,10 @@
 
 def solver(group, j):
     return 2 * j + lax.rem(group + j, 2)
+
+
+def solver_of(group, j):
+    return 2 * j + (group + j) % 2
 
 
 def spot(fk, c, r):
@@ -108,6 +112,12 @@
     right, left = lax.rem(tile + 1, tiles), lax.rem(tile + tiles - 1, tiles)
     for t in (right, left):
         pl.semaphore_signal(barrier, inc=1, device_id=(t, lev), device_id_type=MESH)
+
+    has_previous, has_next = tile != 0, tile != tiles - 1
+    for way, has in ((0, has_previous), (1, has_next)):
+        @pl.when(jnp.logical_not(has))
+        def _():
+            hr[way] = jnp.zeros((2, STACK, LANES), jnp.float32)
 
     def loads(i):
         rows = pl.ds(quarter_row(i), QUARTER)
@@ -302,18 +312,21 @@
 
     lax.fori_loop(0, 2, solve, 0)
 
-    def returned(half):
-        own_backward(half).wait()
-
+    def returned(half, sources):
         def run(part):
-            for off in range(1, N):
-                backward_from(half, lax.rem(lev + off, N), part).wait_recv()
+            for s in sources:
+                pl.when(lev != s)(lambda: backward_from(half, s, part).wait_recv())
 
         by_slab(lev, BACKWARD, run)
-
-    def substitute(half, j):
+        for s in sources:
+            pl.when(lev == s)(lambda: own_backward(half).wait())
+
+    def substitute(half, j, way=None):
         start = pl.multiple_of(quarter_row(half * 2 + lax.div(j, 2)) + 8 * lax.rem(j, 2), 8)
         rows = pl.ds(start, 8)
+        if way is not None:
+            edge = 0 if way else ROWS - 1
+            weight = [s_v[way, edge:edge + 1, c * LANES:(c + 1) * LANES] for c in range(2)]
         for c in range(2):
             cols = pl.ds(c * LANES, LANES)
             source = solver(lax.div(j, 2), 2 * lax.rem(j, 2) + c)
@@ -325,6 +338,9 @@
                     beyond = rtr[half, source, FIELDS + f] if k == LEVELS - 1 else x[f]
                     x[f] = m_v[f, k, rows, cols] + g * u + e * beyond
                     x_v[pl.ds(pl.multiple_of(spot(f * LEVELS + k, c, start), 8), 8), :] = x[f]
+                    if way is not None:
+                        edge = 0 if way else 7
+                        hs[way, c, pl.ds(f * LEVELS + k, 1), :] = x[f][edge:edge + 1, :] * weight[c]
 
     def halo(way):
         to = right if way == 0 else left
@@ -332,9 +348,6 @@
             src_ref=hs.at[way], dst_ref=hr.at[way], send_sem=hss.at[way], recv_sem=hrs.at[way],
             device_id=(to, lev), device_id_type=MESH)
 
-    def every(c, r):
-        return pl.ds(spot(0, c, r), STACK, stride=2 * HEIGHT)
-
     def blocks(half, first, count, step):
         def body(n, carry):
             substitute(half, first + n * step)
@@ -342,20 +355,21 @@
 
         lax.fori_loop(0, count, body, 0, unroll=2)
 
-    returned(0)
-    blocks(0, 0, 2, 3)
-    for way, r in ((0, ROWS - 1), (1, 0)):
-        for c in range(2):
-            weight = s_v[way, r:r + 1, c * LANES:(c + 1) * LANES]
-            hs[way, c] = x_v[every(c, r), :] * weight
-        halo(way).start()
+    for way, j, tiles_of in ((1, 0, (0, 1)), (0, 3, (2, 3))):
+        returned(0, [solver_of(j // 2, n) for n in tiles_of])
+        substitute(0, j, way)
+        has = has_next if way == 0 else has_previous
+        pl.when(has)(lambda: halo(way).start())
+    returned(0, [solver_of(0, 2), solver_of(0, 3), solver_of(1, 0), solver_of(1, 1)])
     blocks(0, 1, 2, 1)
     lax.fori_loop(0, 2, lambda j, carry: transport(x_v, co_v, part, j * (ROWS - QUARTER), j * QUARTER), 0)
-    returned(1)
+    returned(1, range(N))
     blocks(1, 0, 4, 1)
     transport(x_v, co_v, part, QUARTER, 2 * QUARTER)
     for way in range(2):
-        halo(way).wait()
+        to, of = (has_next, has_previous) if way == 0 else (has_previous, has_next)
+        pl.when(of)(lambda: halo(way).wait_recv())
+        pl.when(to)(lambda: halo(way).wait_send())
 
     def drain(part):
         for half in range(2):

time: 26.5 us -> 25.9 us (0.977)
  Pallas kernels: 26.3 us -> 25.8 us
    pallas_call x1, Pallas kernels: 24.7 us -> 24.1 us  [per_device(): pl.pallas_call(kernel, out_shape=[space((STACK * 2 * HEIGHT, LANES), f32)...]
where the time goes in v2:
time: 25.9 us; the launch traced here: 25.8 us
  Pallas kernels  25.8 us (100%)
    pallas_call x1, Pallas kernels, per_device(): pl.pallas_call(kernel, out_shape=[space((STACK * 2 * HEIGHT, LANES), f32)...  24.1 us
    pallas_call x1, Pallas kernels, per_device(): pl.pallas_call(finish, out_shape=jax.ShapeDtypeStruct(adjoint_state.shape...  1.61 us

profile of v2, /device:TPU:1, one launch (start us, length us, event | category | flops | bytes accessed | tf_op | source)
XLA Modules:
  0.0 25.8 jit_solution(9201439780008507047)
XLA Ops:
  0.0 24.1 %shard_map.55 = (f32[7040,128]{1,0:T(8,128)S(1)}, f32[5,2,64,128]{3,2,1,0:T(8,128)S(1)}, f32[2,2,44,128]{3,2,1,0:T(8,128)S(1)}, f32[4,11,48,256]{3,2,1,0:T(8,128)S(1)}) custom-call(f32[4,11,64,256]{3,2,1,0:T(8,128)} %adj.1, f32[11,64,256]{2,1,0:T(8,128)} %low.1, f32[11,64,256]{2,1,0:T(8,128)} %upp.1, f32[4,64,256]{2,1,0:T(8,128)} %sten.1, s32[64,256]{1,0:T(8,128)} %mask.1), custom_call_target="tpu_custom_call" | custom-call | tf_op jit(solution)/shard_map/pallas_call | solution.py:391
  24.2 1.6 %shard_map.56 = f32[4,11,64,256]{3,2,1,0:T(8,128)} custom-call(f32[7040,128]{1,0:T(8,128)S(1)} %get-tuple-element.9.x_v, f32[5,2,64,128]{3,2,1,0:T(8,128)S(1)} %get-tuple-element.10.co_v, f32[2,2,44,128]{3,2,1,0:T(8,128)S(1)} %get-tuple-element.11.hr, f32[4,11,48,256]{3,2,1,0:T(8,128)S(1)} %get-tuple-element.12.part), custom_call_target="tpu_custom_call" | custom-call | tf_op jit(solution)/shard_map/pallas_call | solution.py:427

commit v3 on v2

--- a/solution.py
+++ b/solution.py
@@ -130,7 +130,7 @@
     load_mask = pltpu.make_async_copy(mask, k_v, small_sem.at[0])
     load_sten = pltpu.make_async_copy(sten, s_v, small_sem.at[1])
     load_mask.start()
-    for i in range(4):
+    for i in range(2):
         for c in loads(i):
             c.start()
     load_sten.start()
@@ -149,6 +149,12 @@
     def eliminate(i):
         for c in loads(i):
             c.wait()
+
+        @pl.when(i < 2)
+        def _():
+            for c in loads(i + 2):
+                c.start()
+
         start = quarter_row(i)
         rows = pl.ds(start, QUARTER)
         half, group = lax.div(i, 2), lax.rem(i, 2)

time: 25.9 us -> 25.7 us (level)
  Pallas kernels: 25.8 us -> 25.5 us
where the time goes in v3:
time: 25.7 us; the launch traced here: 25.6 us
  Pallas kernels  25.5 us (99%)
    pallas_call x1, Pallas kernels, per_device(): pl.pallas_call(kernel, out_shape=[space((STACK * 2 * HEIGHT, LANES), f32)...  23.9 us
    pallas_call x1, Pallas kernels, per_device(): pl.pallas_call(finish, out_shape=jax.ShapeDtypeStruct(adjoint_state.shape...  1.61 us

profile of v3, /device:TPU:1, one launch (start us, length us, event | category | flops | bytes accessed | tf_op | source)
XLA Modules:
  0.0 25.6 jit_solution(949294704749614349)
XLA Ops:
  0.0 23.9 %shard_map.55 = (f32[7040,128]{1,0:T(8,128)S(1)}, f32[5,2,64,128]{3,2,1,0:T(8,128)S(1)}, f32[2,2,44,128]{3,2,1,0:T(8,128)S(1)}, f32[4,11,48,256]{3,2,1,0:T(8,128)S(1)}) custom-call(f32[4,11,64,256]{3,2,1,0:T(8,128)} %adj.1, f32[11,64,256]{2,1,0:T(8,128)} %low.1, f32[11,64,256]{2,1,0:T(8,128)} %upp.1, f32[4,64,256]{2,1,0:T(8,128)} %sten.1, s32[64,256]{1,0:T(8,128)} %mask.1), custom_call_target="tpu_custom_call" | custom-call | tf_op jit(solution)/shard_map/pallas_call | solution.py:397
  23.9 1.6 %shard_map.56 = f32[4,11,64,256]{3,2,1,0:T(8,128)} custom-call(f32[7040,128]{1,0:T(8,128)S(1)} %get-tuple-element.9.x_v, f32[5,2,64,128]{3,2,1,0:T(8,128)S(1)} %get-tuple-element.10.co_v, f32[2,2,44,128]{3,2,1,0:T(8,128)S(1)} %get-tuple-element.11.hr, f32[4,11,48,256]{3,2,1,0:T(8,128)S(1)} %get-tuple-element.12.part), custom_call_target="tpu_custom_call" | custom-call | tf_op jit(solution)/shard_map/pallas_call | solution.py:433

commit v4 on v3

--- a/solution.py
+++ b/solution.py
@@ -122,9 +122,9 @@
     def loads(i):
         rows = pl.ds(quarter_row(i), QUARTER)
         return (
-            pltpu.make_async_copy(adj.at[:, :, rows, :], m_v.at[:, :, rows, :], load_sem.at[i, 0]),
             pltpu.make_async_copy(low.at[:, rows, :], a_v.at[:, rows, :], load_sem.at[i, 1]),
             pltpu.make_async_copy(upp.at[:, rows, :], b_v.at[:, rows, :], load_sem.at[i, 2]),
+            pltpu.make_async_copy(adj.at[:, :, rows, :], m_v.at[:, :, rows, :], load_sem.at[i, 0]),
         )
 
     load_mask = pltpu.make_async_copy(mask, k_v, small_sem.at[0])

time: 25.7 us -> 25.7 us (level)
  no operation moved by 1% of the time
where the time goes in v4:
time: 25.7 us; the launch traced here: 25.6 us
  Pallas kernels  25.6 us (100%)
    pallas_call x1, Pallas kernels, per_device(): pl.pallas_call(kernel, out_shape=[space((STACK * 2 * HEIGHT, LANES), f32)...  24 us
    pallas_call x1, Pallas kernels, per_device(): pl.pallas_call(finish, out_shape=jax.ShapeDtypeStruct(adjoint_state.shape...  1.61 us

profile of v4, /device:TPU:1, one launch (start us, length us, event | category | flops | bytes accessed | tf_op | source)
XLA Modules:
  0.0 25.6 jit_solution(14041712602848897332)
XLA Ops:
  0.0 24.0 %shard_map.55 = (f32[7040,128]{1,0:T(8,128)S(1)}, f32[5,2,64,128]{3,2,1,0:T(8,128)S(1)}, f32[2,2,44,128]{3,2,1,0:T(8,128)S(1)}, f32[4,11,48,256]{3,2,1,0:T(8,128)S(1)}) custom-call(f32[4,11,64,256]{3,2,1,0:T(8,128)} %adj.1, f32[11,64,256]{2,1,0:T(8,128)} %low.1, f32[11,64,256]{2,1,0:T(8,128)} %upp.1, f32[4,64,256]{2,1,0:T(8,128)} %sten.1, s32[64,256]{1,0:T(8,128)} %mask.1), custom_call_target="tpu_custom_call" | custom-call | tf_op jit(solution)/shard_map/pallas_call | solution.py:397
  24.0 1.6 %shard_map.56 = f32[4,11,64,256]{3,2,1,0:T(8,128)} custom-call(f32[7040,128]{1,0:T(8,128)S(1)} %get-tuple-element.9.x_v, f32[5,2,64,128]{3,2,1,0:T(8,128)S(1)} %get-tuple-element.10.co_v, f32[2,2,44,128]{3,2,1,0:T(8,128)S(1)} %get-tuple-element.11.hr, f32[4,11,48,256]{3,2,1,0:T(8,128)S(1)} %get-tuple-element.12.part), custom_call_target="tpu_custom_call" | custom-call | tf_op jit(solution)/shard_map/pallas_call | solution.py:433
